TPU v7x, 32 devices: a whole 2x2x4 slice. The times are simulated.
32 devices in a mesh: groups: 2 (over y), ep: 16 (over z, x, core), tp: 1.
Axes of the slice: x: 2, y: 2, z: 4, core: 2. Of those that a mesh axis runs over, the one named last changes fastest.
Arguments:
- tokens: bfloat16 [128, 3584], P(('groups', 'ep')), parts along dimension 0, may hold values from -6 to 6
- routes: int32 [128, 8], P(('groups', 'ep')), parts along dimension 0, may hold values from 0 to 15, all different within a row; in each aligned block of 4 rows (0 to 3, 4 to 7, ...) at most 2 rows name the same one
- route_weights: bfloat16 [128, 8], P(('groups', 'ep')), parts along dimension 0, may hold values from 0.049804688 to 1
- gate_codes: bfloat16 [3584, 32768], P(None, ('ep', 'tp')), may hold values from -8 to 7, as said below
- gate_scales: float32 [28, 32768], P(None, ('ep', 'tp')), may hold values from 0.002 to 0.006
- up_codes: bfloat16 [3584, 32768], P(None, ('ep', 'tp')), may hold values from -8 to 7, as said below
- up_scales: float32 [28, 32768], P(None, ('ep', 'tp')), may hold values from 0.002 to 0.006
- down_codes: bfloat16 [32768, 3584], P(('ep', 'tp')), may hold values from -8 to 7, as said below
- down_scales: float32 [256, 3584], P(('ep', 'tp')), may hold values from 0.003 to 0.008
Outputs:
- mixed: bfloat16 [128, 3584], P(('groups', 'ep'), 'tp'), parts along dimension 0
- hessian: float32 [65536, 2048], P(('groups', 'ep', 'tp')), parts along dimension 0
There are 2 independent parts, one for each index of `groups`. A program takes and returns all parts, laid end to end along the dimension named above; an argument that names none is the same for every part. Nothing has to cross between parts.
Inputs may be any that keep to these rules, and one draw needn't show every extreme that they name: `routes`: each row names 8 different experts. Among the rows of one index of ep no expert is named more than 2 times, a bound that some block reaches. `gate_codes`: integer values. `up_codes`: integer values. `down_codes`: integer values.
All inputs are finite; a program needn't handle non-finite values.
Results may differ from a plain program's by a relative error of at most 0.0072.
Values may be sent and summed in bfloat16 or wider, within the bound.
A program may use at most 128 MiB of HBM per device.

v0:
```python
import jax
import jax.numpy as jnp
from jax import lax
from jax.sharding import PartitionSpec as P

FF = 2048
GROUP = 128


def dequantize(codes, scales):
    height, across = codes.shape
    blocks = codes.astype(jnp.float32).reshape(height // GROUP, GROUP, across) * scales[:, None, :]
    return blocks.reshape(height, across).astype(jnp.bfloat16)


def slot_targets(flat, experts, capacity):
    table = (flat[..., None] == jnp.arange(experts, dtype=jnp.int32)).astype(jnp.int32)
    earlier = jnp.cumsum(table, axis=-2) - table
    return flat * capacity + jnp.sum(earlier * table, axis=-1)


def pack_rows(tokens, targets, places, choose):
    count = places.shape[0]
    select = (targets[None, :] == places[:, None]).astype(jnp.bfloat16)
    select = select.reshape(count, tokens.shape[0], choose).sum(axis=2)
    return jnp.dot(select, tokens, preferred_element_type=jnp.float32).astype(jnp.bfloat16)


def body(
    tokens,
    routes,
    route_weights,
    gate_codes,
    gate_scales,
    up_codes,
    up_scales,
    down_codes,
    down_scales,
):
    ep_size = lax.axis_size("ep")
    tp_size = lax.axis_size("tp")
    rows, width = tokens.shape
    choose = routes.shape[1]
    unit_count = gate_codes.shape[1]
    sharing = FF // (tp_size * unit_count)
    experts = ep_size // sharing
    capacity = min(rows, rows * choose // experts + 2 * (rows // 8))
    w_gate = dequantize(gate_codes, gate_scales)
    w_up = dequantize(up_codes, up_scales)
    w_down = dequantize(down_codes, down_scales)
    targets = slot_targets(routes.reshape(-1), experts, capacity)
    places = jnp.arange(experts * capacity, dtype=jnp.int32)
    packed = pack_rows(tokens, targets, places, choose).reshape(experts, 1, capacity, width)
    packed = jnp.broadcast_to(packed, (experts, sharing, capacity, width)).reshape(
        ep_size, capacity, width
    )
    arrived = lax.all_to_all(packed, "ep", split_axis=0, concat_axis=0, tiled=True)
    rows_in = arrived.reshape(ep_size * capacity, width)
    gate = jnp.dot(rows_in, w_gate, preferred_element_type=jnp.float32)
    up = jnp.dot(rows_in, w_up, preferred_element_type=jnp.float32)
    hidden = (jax.nn.silu(gate) * up).astype(jnp.bfloat16)
    paired = lax.all_gather(hidden, "tp", axis=1, tiled=True)
    hessian = lax.dot_general(
        hidden, paired, (((0,), (0,)), ((), ())), preferred_element_type=jnp.float32
    ) * (2.0 / (rows * ep_size))
    partial_value = jnp.dot(hidden, w_down, preferred_element_type=jnp.float32).astype(jnp.bfloat16)
    returned = lax.all_to_all(
        partial_value.reshape(ep_size, capacity, width),
        "ep",
        split_axis=0,
        concat_axis=0,
        tiled=True,
    )
    slots = jnp.arange(experts * capacity, dtype=jnp.int32)
    spread = (targets[:, None] == slots[None, :]).astype(jnp.float32) * route_weights.reshape(
        -1
    ).astype(jnp.float32)[:, None]
    spread = (
        spread.reshape(rows, choose, experts * capacity)
        .sum(axis=1)
        .reshape(rows, experts, 1, capacity)
    )
    spread = jnp.broadcast_to(spread, (rows, experts, sharing, capacity)).reshape(
        rows, ep_size * capacity
    )
    combined = jnp.dot(
        spread.astype(jnp.bfloat16),
        returned.reshape(ep_size * capacity, width),
        preferred_element_type=jnp.float32,
    )
    mixed = lax.psum_scatter(combined, "tp", scatter_dimension=1, tiled=True).astype(jnp.bfloat16)
    return (mixed, hessian)


def solution(mesh):
    placed = (
        P(("groups", "ep"), None),
        P(("groups", "ep"), None),
        P(("groups", "ep"), None),
        P(None, ("ep", "tp")),
        P(None, ("ep", "tp")),
        P(None, ("ep", "tp")),
        P(None, ("ep", "tp")),
        P(("ep", "tp"), None),
        P(("ep", "tp"), None),
    )
    return jax.shard_map(
        body,
        mesh=mesh,
        in_specs=placed,
        out_specs=(P(("groups", "ep"), "tp"), P(("groups", "ep", "tp"), None)),
        check_vma=False,
    )
```

profile of v0, /device:TPU:0, one launch (start us, length us, event | category | flops | bytes accessed | tf_op | source)
XLA Modules:
  0.0 77.4 jit_solution(10152523939715006625)
XLA Ops:
  0.6 0.0 copy-start
  0.6 0.8 eq.43
  1.4 0.1 fusion.4
  1.5 0.1 reduce_window_sum.11
  1.5 0.2 select_reduce_fusion.1
  1.7 0.1 reduce_sum.33
  1.8 0.7 multiply_add_fusion
  2.5 0.1 fusion.6
  2.6 0.0 copy-done
  2.6 0.3 convolution_convert_fusion.1
  2.9 0.8 %reshape_reshape.3 = bf16[16,2,3584]{2,1,0:T(2,128)(2,1)} reshape(bf16[32,3584]{1,0:T(8,128)(2,1)S(1)} %convolution_convert_fusion.1) | data formatting | bytes 458752 | tf_op jit(solution)/shard_map/reshape;reshape | solution.py:54
  3.7 0.0 slice-start.4
  3.7 7.5 %all-to-all-start = ((bf16[16,2,3584]{2,1,0:T(2,128)(2,1)}), bf16[16,2,3584]{2,1,0:T(2,128)(2,1)S(1)}, u32[]{:S(2)}, u32[]{:S(2)}) async-start(bf16[16,2,3584]{2,1,0:T(2,128)(2,1)} %reshape_reshape.3), calls=%async_computation | async-start | bytes 458752 | tf_op jit(solution)/shard_map/all_to_all | solution.py:57
  11.2 0.7 convert_element_type.51
  11.8 0.0 slice-start.5
  11.8 0.0 slice-start.6
  11.9 0.0 slice-start.7
  11.9 0.0 copy-start.3
  11.9 0.0 slice-start.8
  11.9 0.0 slice-start.9
  11.9 0.0 slice-start.10
  11.9 17.3 %fusion.2 = bf16[3584,2048]{1,0:T(8,128)(2,1)} fusion(bf16[3584,2048]{1,0:T(8,128)(2,1)} %param.12, f32[28,2048]{1,0:T(8,128)} %param.13), kind=kLoop, calls=%fused_computation.5 | loop fusion | flops 22020096 | bytes 29589504 | tf_op jit(solution)/shard_map/convert_element_type | solution.py:13
  29.2 0.0 slice-done.4
  29.2 0.0 slice-done.5
  29.2 0.0 slice-done.6
  29.2 0.0 slice-done.7
  29.2 0.0 copy-done.3
  29.2 0.0 slice-start.11
  29.2 0.0 copy-start.4
  29.3 7.3 %fusion.1 = bf16[3584,2048]{1,0:T(8,128)(2,1)} fusion(bf16[3584,2048]{1,0:T(8,128)(2,1)S(1)} %bitcast.27, f32[28,2048]{1,0:T(8,128)S(1)} %copy-done.3), kind=kLoop, calls=%fused_computation.3 | loop fusion | flops 22020096 | bytes 29589504 | tf_op jit(solution)/shard_map/convert_element_type | solution.py:13
  36.5 0.0 slice-done.8
  36.5 0.0 slice-done.9
  36.5 0.0 slice-done.10
  36.5 0.0 slice-done.11
  36.5 0.0 copy-done.4
  36.6 7.1 %fusion = bf16[2048,3584]{1,0:T(8,128)(2,1)} fusion(bf16[2048,3584]{1,0:T(8,128)(2,1)S(1)} %bitcast.29, f32[16,3584]{1,0:T(8,128)S(1)} %copy-done.4), kind=kLoop, calls=%fused_computation.1 | loop fusion | flops 22020096 | bytes 29589504 | tf_op jit(solution)/shard_map/convert_element_type | solution.py:13
  43.7 0.1 select_reduce_fusion
  43.8 0.0 all-to-all-done
  43.8 0.1 reshape.71
  43.9 0.0 copy-start.2
  43.9 0.0 slice-start
  43.9 0.0 slice-start.1
  43.9 8.0 %fusion.8 = f32[32,2048]{1,0:T(8,128)S(1)} fusion(bf16[32,3584]{1,0:T(8,128)(2,1)S(1)} %reshape.71, bf16[3584,2048]{1,0:T(8,128)(2,1)} %fusion.2), kind=kOutput, calls=%fused_computation.22 | convolution fusion | flops 469762048 | bytes 15171584 | tf_op jit(solution)/shard_map/dot_general | solution.py:59
  52.0 1.3 %copy-done.2 = bf16[3584,2048]{1,0:T(8,128)(2,1)S(1)} copy-done((bf16[3584,2048]{1,0:T(8,128)(2,1)S(1)}, bf16[3584,2048]{1,0:T(8,128)(2,1)}, u32[]{:S(2)}) %copy-start.2) | copy-done | bytes 14680088
  53.3 0.0 slice-start.2
  53.3 0.0 slice-start.3
  53.3 2.7 %fusion.3 = bf16[32,2048]{1,0:T(8,128)(2,1)S(1)} fusion(bf16[32,3584]{1,0:T(8,128)(2,1)S(1)} %reshape.71, bf16[3584,2048]{1,0:T(8,128)(2,1)S(1)} %copy-done.2, f32[32,2048]{1,0:T(8,128)S(1)} %fusion.8), kind=kOutput, calls=%fused_computation.11 | convolution fusion | flops 470155264 | bytes 15302656 | tf_op jit(solution)/shard_map/dot_general | solution.py:60
  56.0 0.0 slice-done
  56.0 0.0 slice-done.1
  56.0 1.1 %slice-done.2 = s8[4194304]{0:T(1024)(128)(4,1)S(1)} async-done(((s8[14680064]{0:T(1024)(128)(4,1)}), s8[4194304]{0:T(1024)(128)(4,1)S(1)}, s32[]{:S(2)}) %slice-start.2) | async-done | bytes 4194328
  57.1 0.6 slice-done.3
  57.7 0.0 copy-start.1
  57.7 2.6 %convolution_convert_fusion = bf16[32,3584]{1,0:T(8,128)(2,1)S(1)} fusion(bf16[32,2048]{1,0:T(8,128)(2,1)S(1)} %fusion.3, bf16[2048,3584]{1,0:T(8,128)(2,1)S(1)} %bitcast.25), kind=kOutput, calls=%fused_computation.7 | convolution fusion | flops 469876736 | bytes 15040512 | tf_op jit(solution)/shard_map/dot_general | solution.py:66
  60.2 0.8 %reshape.72 = bf16[16,2,3584]{2,1,0:T(2,128)(2,1)} reshape(bf16[32,3584]{1,0:T(8,128)(2,1)S(1)} %convolution_convert_fusion) | data formatting | bytes 458752 | tf_op jit(solution)/shard_map/reshape | solution.py:68
  61.0 6.0 %all-to-all-start.1 = ((bf16[16,2,3584]{2,1,0:T(2,128)(2,1)}), bf16[16,2,3584]{2,1,0:T(2,128)(2,1)S(1)}, u32[]{:S(2)}, u32[]{:S(2)}) async-start(bf16[16,2,3584]{2,1,0:T(2,128)(2,1)} %reshape.72), calls=%async_computation.1 | async-start | bytes 458752 | tf_op jit(solution)/shard_map/all_to_all | solution.py:67
  67.0 8.5 %convolution_multiply_fusion = f32[2048,2048]{1,0:T(8,128)} fusion(bf16[32,2048]{1,0:T(8,128)(2,1)S(1)} %fusion.3), kind=kOutput, calls=%fused_computation.6 | convolution fusion | flops 272629760 | bytes 16908288 | tf_op jit(solution)/shard_map/dot_general | solution.py:63
  75.6 1.0 %all-to-all-done.1 = bf16[16,2,3584]{2,1,0:T(2,128)(2,1)S(1)} async-done(((bf16[16,2,3584]{2,1,0:T(2,128)(2,1)}), bf16[16,2,3584]{2,1,0:T(2,128)(2,1)S(1)}, u32[]{:S(2)}, u32[]{:S(2)}) %all-to-all-start.1) | async-done | bytes 229408 | tf_op jit(solution)/shard_map/all_to_all | solution.py:67
  76.6 0.1 reshape.73
  76.7 0.8 convolution_convert_fusion.2
  77.4 0.0 copy-done.1
  (3 shorter events, 0.0 us)
Async XLA Ops:
  0.6 2.0 %copy-start = (bf16[4,3584]{1,0:T(4,128)(2,1)S(1)}, bf16[4,3584]{1,0:T(4,128)(2,1)}, u32[]{:S(2)}) copy-start(bf16[4,3584]{1,0:T(4,128)(2,1)} %param.9) | copy-start | bytes 86020
  3.7 25.5 %slice-start.4 = ((s8[14680064]{0:T(1024)(128)(4,1)}), s8[2097152]{0:T(1024)(128)(4,1)S(1)}, s32[]{:S(2)}) async-start(s8[14680064]{0:T(1024)(128)(4,1)} %bitcast.26), calls=%async_computation.6 | async-start | bytes 4194304
  3.7 40.1 %all-to-all-start = ((bf16[16,2,3584]{2,1,0:T(2,128)(2,1)}), bf16[16,2,3584]{2,1,0:T(2,128)(2,1)S(1)}, u32[]{:S(2)}, u32[]{:S(2)}) async-start(bf16[16,2,3584]{2,1,0:T(2,128)(2,1)} %reshape_reshape.3), calls=%async_computation | async-start | bytes 458752 | tf_op jit(solution)/shard_map/all_to_all | solution.py:57
  11.8 17.3 %slice-start.5 = ((s8[14680064]{0:T(1024)(128)(4,1)}), s8[4194304]{0:T(1024)(128)(4,1)S(1)}, s32[]{:S(2)}) async-start(s8[14680064]{0:T(1024)(128)(4,1)} %bitcast.26), calls=%async_computation.7 | async-start | bytes 8388608
  11.8 17.3 %slice-start.6 = ((s8[14680064]{0:T(1024)(128)(4,1)}), s8[4194304]{0:T(1024)(128)(4,1)S(1)}, s32[]{:S(2)}) async-start(s8[14680064]{0:T(1024)(128)(4,1)} %bitcast.26), calls=%async_computation.8 | async-start | bytes 8388608
  11.9 17.4 %slice-start.7 = ((s8[14680064]{0:T(1024)(128)(4,1)}), s8[4194304]{0:T(1024)(128)(4,1)S(1)}, s32[]{:S(2)}) async-start(s8[14680064]{0:T(1024)(128)(4,1)} %bitcast.26), calls=%async_computation.9 | async-start | bytes 8388608
  11.9 17.4 %copy-start.3 = (f32[28,2048]{1,0:T(8,128)S(1)}, f32[28,2048]{1,0:T(8,128)}, u32[]{:S(2)}) copy-start(f32[28,2048]{1,0:T(8,128)} %param.15) | copy-start | bytes 688132
  11.9 24.7 %slice-start.8 = ((s8[14680064]{0:T(1024)(128)(4,1)}), s8[4194304]{0:T(1024)(128)(4,1)S(1)}, s32[]{:S(2)}) async-start(s8[14680064]{0:T(1024)(128)(4,1)} %bitcast.28), calls=%async_computation.10 | async-start | bytes 8388608
  11.9 24.7 %slice-start.9 = ((s8[14680064]{0:T(1024)(128)(4,1)}), s8[4194304]{0:T(1024)(128)(4,1)S(1)}, s32[]{:S(2)}) async-start(s8[14680064]{0:T(1024)(128)(4,1)} %bitcast.28), calls=%async_computation.11 | async-start | bytes 8388608
  11.9 24.6 %slice-start.10 = ((s8[14680064]{0:T(1024)(128)(4,1)}), s8[4194304]{0:T(1024)(128)(4,1)S(1)}, s32[]{:S(2)}) async-start(s8[14680064]{0:T(1024)(128)(4,1)} %bitcast.28), calls=%async_computation.12 | async-start | bytes 8388608
  29.2 7.3 %slice-start.11 = ((s8[14680064]{0:T(1024)(128)(4,1)}), s8[2097152]{0:T(1024)(128)(4,1)S(1)}, s32[]{:S(2)}) async-start(s8[14680064]{0:T(1024)(128)(4,1)} %bitcast.28), calls=%async_computation.13 | async-start | bytes 4194304
  29.2 7.3 %copy-start.4 = (f32[16,3584]{1,0:T(8,128)S(1)}, f32[16,3584]{1,0:T(8,128)}, u32[]{:S(2)}) copy-start(f32[16,3584]{1,0:T(8,128)} %param.17) | copy-start | bytes 688132
  43.9 9.4 %copy-start.2 = (bf16[3584,2048]{1,0:T(8,128)(2,1)S(1)}, bf16[3584,2048]{1,0:T(8,128)(2,1)}, u32[]{:S(2)}) copy-start(bf16[3584,2048]{1,0:T(8,128)(2,1)} %fusion.1) | copy-start | bytes 44040196
  43.9 12.1 %slice-start = ((s8[14680064]{0:T(1024)(128)(4,1)}), s8[4194304]{0:T(1024)(128)(4,1)S(1)}, s32[]{:S(2)}) async-start(s8[14680064]{0:T(1024)(128)(4,1)} %bitcast.24), calls=%async_computation.2 | async-start | bytes 8388608
  43.9 12.1 %slice-start.1 = ((s8[14680064]{0:T(1024)(128)(4,1)}), s8[4194304]{0:T(1024)(128)(4,1)S(1)}, s32[]{:S(2)}) async-start(s8[14680064]{0:T(1024)(128)(4,1)} %bitcast.24), calls=%async_computation.3 | async-start | bytes 8388608
  53.3 3.8 %slice-start.2 = ((s8[14680064]{0:T(1024)(128)(4,1)}), s8[4194304]{0:T(1024)(128)(4,1)S(1)}, s32[]{:S(2)}) async-start(s8[14680064]{0:T(1024)(128)(4,1)} %bitcast.24), calls=%async_computation.4 | async-start | bytes 8388608
  53.3 4.4 %slice-start.3 = ((s8[14680064]{0:T(1024)(128)(4,1)}), s8[2097152]{0:T(1024)(128)(4,1)S(1)}, s32[]{:S(2)}) async-start(s8[14680064]{0:T(1024)(128)(4,1)} %bitcast.24), calls=%async_computation.5 | async-start | bytes 4194304
  57.7 19.7 %copy-start.1 = (bf16[4,3584]{1,0:T(4,128)(2,1)S(1)}, bf16[4,3584]{1,0:T(4,128)(2,1)}, u32[]{:S(2)}) copy-start(bf16[4,3584]{1,0:T(4,128)(2,1)} %param.9) | copy-start | bytes 86020
  61.0 15.5 %all-to-all-start.1 = ((bf16[16,2,3584]{2,1,0:T(2,128)(2,1)}), bf16[16,2,3584]{2,1,0:T(2,128)(2,1)S(1)}, u32[]{:S(2)}, u32[]{:S(2)}) async-start(bf16[16,2,3584]{2,1,0:T(2,128)(2,1)} %reshape.72), calls=%async_computation.1 | async-start | bytes 458752 | tf_op jit(solution)/shard_map/all_to_all | solution.py:67
where the time goes:
time: 77.9 us; the launch traced here: 77.4 us
  other arithmetic  33.6 us (43%)
  matrix products  22.8 us (29%)
  starting transfers between devices  13.5 us (17%)
  local copies, waits for them, and re-layouts  5.67 us (7%)
  waiting for transfers between devices  0.99 us (1%)
  between operations  0.84 us (1%)
    convert_element_type x3, other arithmetic, dequantize(): return blocks.reshape(height, across).astype(jnp.bfloat16)  31.7 us
    dot_general x1, matrix products, body(): lax.dot_general(hidden, paired, (((0,), (0,)), ((), ())), preferred_eleme...  8.53 us
    dot_general x1, matrix products, body(): gate = jnp.dot(rows_in, w_gate, preferred_element_type=jnp.float32)  8.03 us
    all_to_all x1, starting transfers between devices, body(): lax.all_to_all(packed, 'ep', split_axis=0, concat_axis=0, tiled=True)  7.49 us
    all_to_all x1, starting transfers between devices, body(): lax.all_to_all(partial_value.reshape(ep_size, capacity, width), 'ep', spl...  6.01 us
    unnamed x34, local copies, waits for them, and re-layouts  3.06 us
    dot_general x1, matrix products, body(): up = jnp.dot(rows_in, w_up, preferred_element_type=jnp.float32)  2.7 us
    dot_general x1, matrix products, body(): jnp.dot(hidden, w_down, preferred_element_type=jnp.float32)  2.56 us
  transfers between devices with their start and end apart: 2, of which 1 were waited for; matrix products, arithmetic and copies ran while one was open for 53% of the time, Pallas kernels for 0%

commit v1 on v0

--- a/solution.py
+++ b/solution.py
@@ -1,6 +1,10 @@
+import functools
+
 import jax
 import jax.numpy as jnp
 from jax import lax
+from jax.experimental import pallas as pl
+from jax.experimental.pallas import tpu as pltpu
 from jax.sharding import PartitionSpec as P
 
 FF = 2048
@@ -92,6 +96,297 @@
     return (mixed, hessian)
 
 
+STAGE = 512
+WIDE = 256
+PAIR = 2 * GROUP
+
+
+def pieces(total, parts):
+    parts = min(parts, total)
+    counts = [total // parts + (1 if i < total % parts else 0) for i in range(parts)]
+    return [(sum(counts[:i]), counts[i]) for i in range(parts)]
+
+
+def moe_kernel(
+    plan,
+    tokens,
+    routes,
+    route_weights,
+    gate_codes,
+    gate_scales,
+    up_codes,
+    up_scales,
+    down_codes,
+    down_scales,
+    mixed,
+    hidden_out,
+    gate_v,
+    up_v,
+    down_v,
+    gate_s,
+    up_s,
+    down_s,
+    gate_acc,
+    up_acc,
+    lhs,
+    lhs_down,
+    *rest,
+):
+    ep_size, slots, out_parts, back_parts = plan
+    nd, nb = len(out_parts), len(back_parts)
+    sends, recvs = rest[:nd], rest[nd : 2 * nd]
+    psends, precvs = rest[2 * nd : 2 * nd + nb], rest[2 * nd + nb : 2 * nd + 2 * nb]
+    scale_sem, gate_sem, up_sem, down_sem, out_send, out_recv, back_send, back_recv = rest[2 * nd + 2 * nb :]
+    me = lax.axis_index("ep")
+    width, units = gate_v.shape
+    rows = ep_size * slots
+    toks = tokens.shape[0]
+    stages = width // STAGE
+    downs = down_v.shape[1] // STAGE
+
+    def peer(off):
+        return {"ep": lax.rem(me + off, ep_size)}
+
+    barrier = pltpu.get_barrier_semaphore()
+    for off in range(1, ep_size):
+        pl.semaphore_signal(barrier, inc=1, device_id=peer(off), device_id_type=pl.DeviceIdType.MESH)
+
+    scale_loads = [
+        pltpu.make_async_copy(gate_scales, gate_s, scale_sem.at[0]),
+        pltpu.make_async_copy(up_scales, up_s, scale_sem.at[1]),
+        pltpu.make_async_copy(down_scales, down_s, scale_sem.at[2]),
+    ]
+    gate_loads, up_loads, down_loads = [], [], []
+    for st in range(stages):
+        part = pl.ds(st * STAGE, STAGE)
+        gate_loads.append(pltpu.make_async_copy(gate_codes.at[part], gate_v.at[part], gate_sem.at[st]))
+        up_loads.append(pltpu.make_async_copy(up_codes.at[part], up_v.at[part], up_sem.at[st]))
+    for st in range(downs):
+        part = pl.ds(st * STAGE, STAGE)
+        down_loads.append(pltpu.make_async_copy(down_codes.at[:, part], down_v.at[:, part], down_sem.at[st]))
+    scale_loads[0].start()
+    scale_loads[1].start()
+    for st in range(stages):
+        gate_loads[st].start()
+        up_loads[st].start()
+    scale_loads[2].start()
+    for load in down_loads:
+        load.start()
+
+    row = lax.broadcasted_iota(jnp.int32, (rows, routes.shape[1]), 0)
+    expert = lax.rem(me + row // slots, ep_size)
+    slot = (row - (row // slots) * slots)[:, :1].astype(jnp.float32)
+    seen = jnp.zeros((rows, 1), jnp.float32)
+    chosen, factors = [], []
+    for t in range(toks):
+        hit = (routes[t : t + 1, :] == expert).astype(jnp.float32)
+        named = jnp.sum(hit, axis=1, keepdims=True)
+        take = named * (seen == slot).astype(jnp.float32)
+        weight = jnp.sum(hit * route_weights[t : t + 1, :].astype(jnp.float32), axis=1, keepdims=True)
+        chosen.append(take)
+        factors.append(take * weight)
+        seen = seen + named
+
+    for c, (first, count) in enumerate(out_parts):
+        for st in range(count):
+            lo = (first + st) * STAGE
+            value = chosen[0] * tokens[0:1, lo : lo + STAGE].astype(jnp.float32)
+            for t in range(1, toks):
+                value = value + chosen[t] * tokens[t : t + 1, lo : lo + STAGE].astype(jnp.float32)
+            value = value.reshape(ep_size, slots, STAGE).astype(jnp.bfloat16)
+            sends[c][:, :, st * STAGE : (st + 1) * STAGE] = value
+
+    pl.semaphore_wait(barrier, ep_size - 1)
+
+    def exchange(source, target, send_sem, recv_sem, c, sign):
+        copies = []
+        for off in range(1, ep_size):
+            copies.append(
+                pltpu.make_async_remote_copy(
+                    src_ref=source.at[off],
+                    dst_ref=target.at[off],
+                    send_sem=send_sem.at[c, off],
+                    recv_sem=recv_sem.at[c, off],
+                    device_id=peer(off if sign > 0 else ep_size - off),
+                    device_id_type=pl.DeviceIdType.MESH,
+                )
+            )
+        for copy in copies:
+            copy.start()
+        return copies
+
+    moves = [exchange(sends[c], recvs[c], out_send, out_recv, c, 1) for c in range(nd)]
+
+    lhs[...] = jnp.zeros_like(lhs)
+    lhs_down[...] = jnp.zeros_like(lhs_down)
+    scale_loads[0].wait()
+    scale_loads[1].wait()
+
+    for c, (first, count) in enumerate(out_parts):
+        recvs[c][0] = sends[c][0]
+        for copy in moves[c]:
+            copy.wait_recv()
+        for st in range(first, first + count):
+            block = recvs[c][:, :, (st - first) * STAGE : (st - first + 1) * STAGE]
+            block = block.astype(jnp.float32).reshape(rows, STAGE).astype(jnp.bfloat16)
+            pairs = STAGE // PAIR
+            for p in range(pairs):
+                lhs[st * pairs + p, :rows, :GROUP] = block[:, p * PAIR : p * PAIR + GROUP]
+                lhs[st * pairs + p, rows:, GROUP:] = block[:, p * PAIR + GROUP : (p + 1) * PAIR]
+            gate_loads[st].wait()
+            up_loads[st].wait()
+
+            def columns(n, _, st=st, pairs=pairs):
+                cols = pl.ds(pl.multiple_of(n * WIDE, WIDE), WIDE)
+                for codes, scales, acc in ((gate_v, gate_s, gate_acc), (up_v, up_s, up_acc)):
+                    total = None if st == 0 else acc[:, cols]
+                    for p in range(pairs):
+                        at = st * pairs + p
+                        got = jnp.dot(
+                            lhs[at], codes[at * PAIR : (at + 1) * PAIR, cols], preferred_element_type=jnp.float32
+                        )
+                        term = got[:rows] * scales[2 * at : 2 * at + 1, cols]
+                        term = term + got[rows:] * scales[2 * at + 1 : 2 * at + 2, cols]
+                        total = term if total is None else total + term
+                    acc[:, cols] = total
+                return 0
+
+            lax.fori_loop(0, units // WIDE, columns, 0)
+
+    for p in range(units // PAIR):
+        gate = gate_acc[:, p * PAIR : (p + 1) * PAIR]
+        up = up_acc[:, p * PAIR : (p + 1) * PAIR]
+        value = (jax.nn.silu(gate) * up).astype(jnp.bfloat16)
+        hidden_out[:, p * PAIR : (p + 1) * PAIR] = value
+        lhs_down[p, :rows, :GROUP] = value[:, :GROUP]
+        lhs_down[p, rows:, GROUP:] = value[:, GROUP:]
+
+    scale_loads[2].wait()
+    backs = []
+    for c, (first, count) in enumerate(back_parts):
+        for st in range(first, first + count):
+            down_loads[st].wait()
+            for n in range(STAGE // WIDE):
+                lo = st * STAGE + n * WIDE
+                total = None
+                for at in range(units // PAIR):
+                    got = jnp.dot(
+                        lhs_down[at],
+                        down_v[at * PAIR : (at + 1) * PAIR, lo : lo + WIDE],
+                        preferred_element_type=jnp.float32,
+                    )
+                    term = got[:rows] * down_s[2 * at : 2 * at + 1, lo : lo + WIDE]
+                    term = term + got[rows:] * down_s[2 * at + 1 : 2 * at + 2, lo : lo + WIDE]
+                    total = term if total is None else total + term
+                here = lo - first * STAGE
+                psends[c][:, :, here : here + WIDE] = total.reshape(ep_size, slots, WIDE).astype(jnp.bfloat16)
+        backs.append(exchange(psends[c], precvs[c], back_send, back_recv, c, -1))
+
+    for c, (first, count) in enumerate(back_parts):
+        precvs[c][0] = psends[c][0]
+        for copy in backs[c]:
+            copy.wait_recv()
+        for st in range(count):
+            value = precvs[c][:, :, st * STAGE : (st + 1) * STAGE].astype(jnp.float32).reshape(rows, STAGE)
+            lo = (first + st) * STAGE
+            for t in range(toks):
+                total = jnp.sum(value * factors[t], axis=0, keepdims=True)
+                mixed[t : t + 1, lo : lo + STAGE] = total.astype(jnp.bfloat16)
+
+    for copies in moves + backs:
+        for copy in copies:
+            copy.wait_send()
+
+
+def hessian_kernel(factor, left, right, out):
+    out[...] = (
+        lax.dot_general(left[...], right[...], (((0,), (0,)), ((), ())), preferred_element_type=jnp.float32) * factor
+    )
+
+
+def fused_body(*args):
+    tokens, routes, route_weights, gate_codes, gate_scales, up_codes, up_scales, down_codes, down_scales = args
+    ep_size = lax.axis_size("ep")
+    toks, width = tokens.shape
+    units = gate_codes.shape[1]
+    slots = toks * routes.shape[1] // ep_size
+    rows = ep_size * slots
+    out_parts = pieces(width // STAGE, 2)
+    back_parts = pieces(width // STAGE, 3)
+    nd, nb = len(out_parts), len(back_parts)
+    slabs = [pltpu.VMEM((ep_size, slots, count * STAGE), jnp.bfloat16) for _, count in out_parts]
+    back_slabs = [pltpu.VMEM((ep_size, slots, count * STAGE), jnp.bfloat16) for _, count in back_parts]
+    stages = width // STAGE
+    whole = pl.BlockSpec(memory_space=pltpu.VMEM)
+    far = pl.BlockSpec(memory_space=pl.ANY)
+    mixed, hidden = pl.pallas_call(
+        functools.partial(moe_kernel, (ep_size, slots, out_parts, back_parts)),
+        out_shape=(
+            jax.ShapeDtypeStruct((toks, width), jnp.bfloat16),
+            jax.ShapeDtypeStruct((rows, units), jnp.bfloat16),
+        ),
+        in_specs=[whole] * 3 + [far] * 6,
+        out_specs=(whole, whole),
+        scratch_shapes=[
+            pltpu.VMEM(gate_codes.shape, jnp.bfloat16),
+            pltpu.VMEM(up_codes.shape, jnp.bfloat16),
+            pltpu.VMEM(down_codes.shape, jnp.bfloat16),
+            pltpu.VMEM(gate_scales.shape, jnp.float32),
+            pltpu.VMEM(up_scales.shape, jnp.float32),
+            pltpu.VMEM(down_scales.shape, jnp.float32),
+            pltpu.VMEM((rows, units), jnp.float32),
+            pltpu.VMEM((rows, units), jnp.float32),
+            pltpu.VMEM((width // PAIR, 2 * rows, PAIR), jnp.bfloat16),
+            pltpu.VMEM((units // PAIR, 2 * rows, PAIR), jnp.bfloat16),
+            *slabs,
+            *slabs,
+            *back_slabs,
+            *back_slabs,
+            pltpu.SemaphoreType.DMA((3,)),
+            pltpu.SemaphoreType.DMA((stages,)),
+            pltpu.SemaphoreType.DMA((stages,)),
+            pltpu.SemaphoreType.DMA((stages,)),
+            pltpu.SemaphoreType.DMA((nd, ep_size)),
+            pltpu.SemaphoreType.DMA((nd, ep_size)),
+            pltpu.SemaphoreType.DMA((nb, ep_size)),
+            pltpu.SemaphoreType.DMA((nb, ep_size)),
+        ],
+        compiler_params=pltpu.CompilerParams(
+            collective_id=0, has_side_effects=True, vmem_limit_bytes=58 * 2**20
+        ),
+        name="moe",
+    )(tokens, routes, route_weights, gate_codes, gate_scales, up_codes, up_scales, down_codes, down_scales)
+    block = 256
+    hessian = pl.pallas_call(
+        functools.partial(hessian_kernel, 2.0 / (toks * ep_size)),
+        out_shape=jax.ShapeDtypeStruct((units, units), jnp.float32),
+        grid=(units // block,),
+        in_specs=[
+            pl.BlockSpec((rows, block), lambda i: (0, i)),
+            pl.BlockSpec((rows, units), lambda i: (0, 0)),
+        ],
+        out_specs=pl.BlockSpec((block, units), lambda i: (i, 0)),
+        compiler_params=pltpu.CompilerParams(vmem_limit_bytes=32 * 2**20),
+        name="hessian",
+    )(hidden, hidden)
+    return (mixed, hessian)
+
+
+def fits(mesh, tokens, routes, gate_codes, down_codes):
+    ep_size = mesh.shape["ep"]
+    toks = tokens.shape[0] // (mesh.shape["groups"] * ep_size)
+    units = gate_codes.shape[1] // (ep_size * mesh.shape["tp"])
+    asked = toks * routes.shape[1]
+    rows_limit = min(toks, asked // ep_size + 2 * (toks // 8))
+    return (
+        mesh.shape["tp"] == 1
+        and units == FF
+        and asked == ep_size * rows_limit
+        and tokens.shape[1] % STAGE == 0
+        and units % STAGE == 0
+    )
+
+
 def solution(mesh):
     placed = (
         P(("groups", "ep"), None),
@@ -104,10 +399,15 @@
         P(("ep", "tp"), None),
         P(("ep", "tp"), None),
     )
-    return jax.shard_map(
-        body,
-        mesh=mesh,
-        in_specs=placed,
-        out_specs=(P(("groups", "ep"), "tp"), P(("groups", "ep", "tp"), None)),
-        check_vma=False,
-    )
+
+    def run(*args):
+        fused = fits(mesh, args[0], args[1], args[3], args[7])
+        return jax.shard_map(
+            fused_body if fused else body,
+            mesh=mesh,
+            in_specs=placed,
+            out_specs=(P(("groups", "ep"), "tp"), P(("groups", "ep", "tp"), None)),
+            check_vma=False,
+        )(*args)
+
+    return run

time: 77.9 us -> 48.5 us (0.62)
  Pallas kernels: 0 us -> 46.2 us
  other arithmetic: 33.6 us -> 0 us
  matrix products: 22.8 us -> 0 us
  starting transfers between devices: 13.5 us -> 0 us
  local copies, waits for them, and re-layouts: 5.67 us -> 1.51 us
  waiting for transfers between devices: 0.99 us -> 0 us
    pallas_call x0 -> x2, Pallas kernels: none -> 46.2 us  [the longest x1 38.4 us: fused_body(): pl.pallas_call(functools.partial(moe_kernel, (ep_size, slots, out_parts,...]
    convert_element_type x5 -> x0, other arithmetic: 32.5 us -> none  [the longest x3 31.7 us: dequantize(): return blocks.reshape(height, across).astype(jnp.bfloat16)]
    dot_general x6 -> x0, matrix products: 22.8 us -> none  [the longest x1 8.53 us: body(): lax.dot_general(hidden, paired, (((0,), (0,)), ((), ())), preferred_eleme...]
    all_to_all x2 -> x0, starting transfers between devices: 13.5 us -> none  [the longest x1 7.49 us: body(): lax.all_to_all(packed, 'ep', split_axis=0, concat_axis=0, tiled=True)]
    unnamed x34 -> x5, local copies, waits for them, and re-layouts: 3.06 us -> 1.51 us
    all_to_all x2 -> x0, waiting for transfers between devices: 0.99 us -> none  [the longest x1 0.99 us: body(): lax.all_to_all(partial_value.reshape(ep_size, capacity, width), 'ep', spl...]
    reshape x3 -> x0, local copies, waits for them, and re-layouts: 0.96 us -> none  [the longest x1 0.79 us: body(): partial_value.reshape(ep_size, capacity, width)]
    another operation x1 -> x0, local copies, waits for them, and re-layouts: 0.79 us -> none  [body(): jnp.broadcast_to(packed, (experts, sharing, capacity, width))]
  transfers between devices with their start and end apart: 2 -> 0, of which waited for: 1 -> 0; matrix products, arithmetic and copies ran while one was open for 53% -> 0% of each run, Pallas kernels for 0% -> 0%
where the time goes in v1:
time: 48.5 us; the launch traced here: 48.3 us
  Pallas kernels  46.2 us (95%)
  local copies, waits for them, and re-layouts  1.51 us (3%)
  between operations  0.65 us (1%)
    pallas_call x1, Pallas kernels, fused_body(): pl.pallas_call(functools.partial(moe_kernel, (ep_size, slots, out_parts,...  38.4 us
    pallas_call x1, Pallas kernels, fused_body(): pl.pallas_call(functools.partial(hessian_kernel, 2.0 / (toks * ep_size)),...  7.81 us
    unnamed x5, local copies, waits for them, and re-layouts  1.51 us

profile of v1, /device:TPU:0, one launch (start us, length us, event | category | flops | bytes accessed | tf_op | source)
XLA Modules:
  0.0 48.3 jit_solution(5781370247477793060)
XLA Ops:
  0.6 38.4 %moe.1 = (bf16[4,3584]{1,0:T(4,128)(2,1)}, bf16[32,2048]{1,0:T(8,128)(2,1)}) custom-call(bf16[4,3584]{1,0:T(4,128)(2,1)} %tokens.1, s32[4,8]{1,0:T(4,128)} %routes.1, bf16[4,8]{1,0:T(4,128)(2,1)} %route_weights.1, bf16[3584,2048]{1,0:T(8,128)(2,1)} %gate_codes.1, f32[28,2048]{1,0:T(8,128)} %gate_scales.1, bf16[3584,2048]{1,0:T(8,128)(2,1)} %up_codes.1, ...), custom_call_target="tpu_custom_call" | custom-call | tf_op jit(solution)/shard_map/moe/pallas_call | solution.py:322
  39.0 0.0 copy-start
  39.0 0.9 %copy-done = bf16[32,2048]{1,0:T(8,128)(2,1)S(1)} copy-done((bf16[32,2048]{1,0:T(8,128)(2,1)S(1)}, bf16[32,2048]{1,0:T(8,128)(2,1)}, u32[]{:S(2)}) %copy-start) | copy-done | bytes 131096
  39.9 0.0 copy-start.1
  39.9 7.8 %hessian.1 = f32[2048,2048]{1,0:T(8,128)} custom-call(bf16[32,2048]{1,0:T(8,128)(2,1)S(1)} %copy-done, bf16[32,2048]{1,0:T(8,128)(2,1)S(1)} %copy-done), custom_call_target="tpu_custom_call" | custom-call | tf_op jit(solution)/shard_map/hessian/pallas_call | solution.py:360
  47.7 0.0 copy-done.1
  47.7 0.6 %copy.12 = bf16[4,3584]{1,0:T(4,128)(2,1)} copy(bf16[4,3584]{1,0:T(4,128)(2,1)S(1)} %copy-done.1) | data formatting | bytes 57344
Async XLA Ops:
  39.0 0.9 %copy-start = (bf16[32,2048]{1,0:T(8,128)(2,1)S(1)}, bf16[32,2048]{1,0:T(8,128)(2,1)}, u32[]{:S(2)}) copy-start(bf16[32,2048]{1,0:T(8,128)(2,1)} %get-tuple-element.5.left.right) | copy-start | bytes 393220
  39.9 7.8 %copy-start.1 = (bf16[4,3584]{1,0:T(4,128)(2,1)S(1)}, bf16[4,3584]{1,0:T(4,128)(2,1)}, u32[]{:S(2)}) copy-start(bf16[4,3584]{1,0:T(4,128)(2,1)} %get-tuple-element.8) | copy-start | bytes 86020

commit v2 on v1

--- a/solution.py
+++ b/solution.py
@@ -1,4 +1,5 @@
 import functools
+import math
 
 import jax
 import jax.numpy as jnp
@@ -243,15 +244,18 @@
                     for p in range(pairs):
                         at = st * pairs + p
                         got = jnp.dot(
-                            lhs[at], codes[at * PAIR : (at + 1) * PAIR, cols], preferred_element_type=jnp.float32
+                            lhs[at, :rows, :GROUP], codes[at * PAIR : at * PAIR + GROUP, cols], preferred_element_type=jnp.float32
                         )
-                        term = got[:rows] * scales[2 * at : 2 * at + 1, cols]
-                        term = term + got[rows:] * scales[2 * at + 1 : 2 * at + 2, cols]
+                        got2 = jnp.dot(
+                            lhs[at, rows:, GROUP:], codes[at * PAIR + GROUP: (at + 1) * PAIR, cols], preferred_element_type=jnp.float32
+                        )
+                        term = got * scales[2 * at : 2 * at + 1, cols]
+                        term = term + got2 * scales[2 * at + 1 : 2 * at + 2, cols]
                         total = term if total is None else total + term
                     acc[:, cols] = total
                 return 0
 
-            lax.fori_loop(0, units // WIDE, columns, 0)
+            lax.fori_loop(0, units // WIDE, columns, 0, unroll=4)
 
     for p in range(units // PAIR):
         gate = gate_acc[:, p * PAIR : (p + 1) * PAIR]
@@ -271,12 +275,17 @@
                 total = None
                 for at in range(units // PAIR):
                     got = jnp.dot(
-                        lhs_down[at],
-                        down_v[at * PAIR : (at + 1) * PAIR, lo : lo + WIDE],
+                        lhs_down[at, :rows, :GROUP],
+                        down_v[at * PAIR : at * PAIR + GROUP, lo : lo + WIDE],
                         preferred_element_type=jnp.float32,
                     )
-                    term = got[:rows] * down_s[2 * at : 2 * at + 1, lo : lo + WIDE]
-                    term = term + got[rows:] * down_s[2 * at + 1 : 2 * at + 2, lo : lo + WIDE]
+                    got2 = jnp.dot(
+                        lhs_down[at, rows:, GROUP:],
+                        down_v[at * PAIR + GROUP: (at + 1) * PAIR, lo : lo + WIDE],
+                        preferred_element_type=jnp.float32,
+                    )
+                    term = got * down_s[2 * at : 2 * at + 1, lo : lo + WIDE]
+                    term = term + got2 * down_s[2 * at + 1 : 2 * at + 2, lo : lo + WIDE]
                     total = term if total is None else total + term
                 here = lo - first * STAGE
                 psends[c][:, :, here : here + WIDE] = total.reshape(ep_size, slots, WIDE).astype(jnp.bfloat16)
@@ -298,10 +307,17 @@
             copy.wait_send()
 
 
-def hessian_kernel(factor, left, right, out):
-    out[...] = (
-        lax.dot_general(left[...], right[...], (((0,), (0,)), ((), ())), preferred_element_type=jnp.float32) * factor
-    )
+def hessian_kernel(factor, hidden, out, held, sem):
+    rows = held.shape[0] // sem.shape[0]
+    copies = []
+    for i in range(sem.shape[0]):
+        part = pl.ds(i * rows, rows)
+        scaled = (hidden[:, i * rows : (i + 1) * rows].astype(jnp.float32) * factor).astype(jnp.bfloat16)
+        held[part] = lax.dot_general(scaled, hidden[...], (((0,), (0,)), ((), ())), preferred_element_type=jnp.float32)
+        copies.append(pltpu.make_async_copy(held.at[part], out.at[part], sem.at[i]))
+        copies[-1].start()
+    for copy in copies:
+        copy.wait()
 
 
 def fused_body(*args):
@@ -356,19 +372,16 @@
         ),
         name="moe",
     )(tokens, routes, route_weights, gate_codes, gate_scales, up_codes, up_scales, down_codes, down_scales)
-    block = 256
+    block = 128
     hessian = pl.pallas_call(
         functools.partial(hessian_kernel, 2.0 / (toks * ep_size)),
         out_shape=jax.ShapeDtypeStruct((units, units), jnp.float32),
-        grid=(units // block,),
-        in_specs=[
-            pl.BlockSpec((rows, block), lambda i: (0, i)),
-            pl.BlockSpec((rows, units), lambda i: (0, 0)),
-        ],
-        out_specs=pl.BlockSpec((block, units), lambda i: (i, 0)),
+        in_specs=[whole],
+        out_specs=far,
+        scratch_shapes=[pltpu.VMEM((units, units), jnp.float32), pltpu.SemaphoreType.DMA((units // block,))],
         compiler_params=pltpu.CompilerParams(vmem_limit_bytes=32 * 2**20),
         name="hessian",
-    )(hidden, hidden)
+    )(hidden)
     return (mixed, hessian)
 
 
@@ -384,6 +397,7 @@
         and asked == ep_size * rows_limit
         and tokens.shape[1] % STAGE == 0
         and units % STAGE == 0
+        and math.frexp(toks * ep_size)[0] == 0.5
     )
 
 

time: 48.5 us -> 40.8 us (0.84)
  Pallas kernels: 46.2 us -> 38.5 us
    pallas_call x1, Pallas kernels: 38.4 us -> 32.2 us  [fused_body(): pl.pallas_call(functools.partial(moe_kernel, (ep_size, slots, out_parts,...]
    pallas_call x1, Pallas kernels: 7.81 us -> 6.28 us  [fused_body(): pl.pallas_call(functools.partial(hessian_kernel, 2.0 / (toks * ep_size)),...]
where the time goes in v2:
time: 40.8 us; the launch traced here: 40.6 us
  Pallas kernels  38.5 us (94%)
  local copies, waits for them, and re-layouts  1.51 us (4%)
  between operations  0.67 us (2%)
    pallas_call x1, Pallas kernels, fused_body(): pl.pallas_call(functools.partial(moe_kernel, (ep_size, slots, out_parts,...  32.2 us
    pallas_call x1, Pallas kernels, fused_body(): pl.pallas_call(functools.partial(hessian_kernel, 2.0 / (toks * ep_size)),...  6.28 us
    unnamed x5, local copies, waits for them, and re-layouts  1.51 us

profile of v2, /device:TPU:0, one launch (start us, length us, event | category | flops | bytes accessed | tf_op | source)
XLA Modules:
  0.0 40.6 jit_solution(6505843722093329086)
XLA Ops:
  0.6 32.2 %moe.1 = (bf16[4,3584]{1,0:T(4,128)(2,1)}, bf16[32,2048]{1,0:T(8,128)(2,1)}) custom-call(bf16[4,3584]{1,0:T(4,128)(2,1)} %tokens.1, s32[4,8]{1,0:T(4,128)} %routes.1, bf16[4,8]{1,0:T(4,128)(2,1)} %route_weights.1, bf16[3584,2048]{1,0:T(8,128)(2,1)} %gate_codes.1, f32[28,2048]{1,0:T(8,128)} %gate_scales.1, bf16[3584,2048]{1,0:T(8,128)(2,1)} %up_codes.1, ...), custom_call_target="tpu_custom_call" | custom-call | tf_op jit(solution)/shard_map/moe/pallas_call | solution.py:338
  32.8 0.0 copy-start
  32.8 0.9 %copy-done = bf16[32,2048]{1,0:T(8,128)(2,1)S(1)} copy-done((bf16[32,2048]{1,0:T(8,128)(2,1)S(1)}, bf16[32,2048]{1,0:T(8,128)(2,1)}, u32[]{:S(2)}) %copy-start) | copy-done | bytes 131096
  33.7 0.0 copy-start.1
  33.7 6.3 %hessian.1 = f32[2048,2048]{1,0:T(8,128)} custom-call(bf16[32,2048]{1,0:T(8,128)(2,1)S(1)} %copy-done), custom_call_target="tpu_custom_call" | custom-call | tf_op jit(solution)/shard_map/hessian/pallas_call | solution.py:376
  40.0 0.0 copy-done.1
  40.0 0.6 %copy.12 = bf16[4,3584]{1,0:T(4,128)(2,1)} copy(bf16[4,3584]{1,0:T(4,128)(2,1)S(1)} %copy-done.1) | data formatting | bytes 57344
Async XLA Ops:
  32.8 0.9 %copy-start = (bf16[32,2048]{1,0:T(8,128)(2,1)S(1)}, bf16[32,2048]{1,0:T(8,128)(2,1)}, u32[]{:S(2)}) copy-start(bf16[32,2048]{1,0:T(8,128)(2,1)} %get-tuple-element.5.hidden) | copy-start | bytes 393220
  33.7 6.3 %copy-start.1 = (bf16[4,3584]{1,0:T(4,128)(2,1)S(1)}, bf16[4,3584]{1,0:T(4,128)(2,1)}, u32[]{:S(2)}) copy-start(bf16[4,3584]{1,0:T(4,128)(2,1)} %get-tuple-element.8) | copy-start | bytes 86020

commit v3 on v2

--- a/solution.py
+++ b/solution.py
@@ -218,8 +218,6 @@
 
     moves = [exchange(sends[c], recvs[c], out_send, out_recv, c, 1) for c in range(nd)]
 
-    lhs[...] = jnp.zeros_like(lhs)
-    lhs_down[...] = jnp.zeros_like(lhs_down)
     scale_loads[0].wait()
     scale_loads[1].wait()
 
@@ -327,8 +325,8 @@
     units = gate_codes.shape[1]
     slots = toks * routes.shape[1] // ep_size
     rows = ep_size * slots
-    out_parts = pieces(width // STAGE, 2)
-    back_parts = pieces(width // STAGE, 3)
+    out_parts = pieces(width // STAGE, 1)
+    back_parts = pieces(width // STAGE, 4)
     nd, nb = len(out_parts), len(back_parts)
     slabs = [pltpu.VMEM((ep_size, slots, count * STAGE), jnp.bfloat16) for _, count in out_parts]
     back_slabs = [pltpu.VMEM((ep_size, slots, count * STAGE), jnp.bfloat16) for _, count in back_parts]

time: 40.8 us -> 40.5 us (level)
  no operation moved by 1% of the time
where the time goes in v3:
time: 40.5 us; the launch traced here: 40.3 us
  Pallas kernels  38.1 us (94%)
  local copies, waits for them, and re-layouts  1.51 us (4%)
  between operations  0.67 us (2%)
    pallas_call x1, Pallas kernels, fused_body(): pl.pallas_call(functools.partial(moe_kernel, (ep_size, slots, out_parts,...  31.9 us
    pallas_call x1, Pallas kernels, fused_body(): pl.pallas_call(functools.partial(hessian_kernel, 2.0 / (toks * ep_size)),...  6.28 us
    unnamed x5, local copies, waits for them, and re-layouts  1.51 us

profile of v3, /device:TPU:0, one launch (start us, length us, event | category | flops | bytes accessed | tf_op | source)
XLA Modules:
  0.0 40.3 jit_solution(13206141276649652855)
XLA Ops:
  0.6 31.9 %moe.1 = (bf16[4,3584]{1,0:T(4,128)(2,1)}, bf16[32,2048]{1,0:T(8,128)(2,1)}) custom-call(bf16[4,3584]{1,0:T(4,128)(2,1)} %tokens.1, s32[4,8]{1,0:T(4,128)} %routes.1, bf16[4,8]{1,0:T(4,128)(2,1)} %route_weights.1, bf16[3584,2048]{1,0:T(8,128)(2,1)} %gate_codes.1, f32[28,2048]{1,0:T(8,128)} %gate_scales.1, bf16[3584,2048]{1,0:T(8,128)(2,1)} %up_codes.1, ...), custom_call_target="tpu_custom_call" | custom-call | tf_op jit(solution)/shard_map/moe/pallas_call | solution.py:336
  32.5 0.0 copy-start
  32.5 0.9 %copy-done = bf16[32,2048]{1,0:T(8,128)(2,1)S(1)} copy-done((bf16[32,2048]{1,0:T(8,128)(2,1)S(1)}, bf16[32,2048]{1,0:T(8,128)(2,1)}, u32[]{:S(2)}) %copy-start) | copy-done | bytes 131096
  33.4 0.0 copy-start.1
  33.4 6.3 %hessian.1 = f32[2048,2048]{1,0:T(8,128)} custom-call(bf16[32,2048]{1,0:T(8,128)(2,1)S(1)} %copy-done), custom_call_target="tpu_custom_call" | custom-call | tf_op jit(solution)/shard_map/hessian/pallas_call | solution.py:374
  39.7 0.0 copy-done.1
  39.7 0.6 %copy.12 = bf16[4,3584]{1,0:T(4,128)(2,1)} copy(bf16[4,3584]{1,0:T(4,128)(2,1)S(1)} %copy-done.1) | data formatting | bytes 57344
Async XLA Ops:
  32.5 0.9 %copy-start = (bf16[32,2048]{1,0:T(8,128)(2,1)S(1)}, bf16[32,2048]{1,0:T(8,128)(2,1)}, u32[]{:S(2)}) copy-start(bf16[32,2048]{1,0:T(8,128)(2,1)} %get-tuple-element.5.hidden) | copy-start | bytes 393220
  33.4 6.3 %copy-start.1 = (bf16[4,3584]{1,0:T(4,128)(2,1)S(1)}, bf16[4,3584]{1,0:T(4,128)(2,1)}, u32[]{:S(2)}) copy-start(bf16[4,3584]{1,0:T(4,128)(2,1)} %get-tuple-element.8) | copy-start | bytes 86020
